TPU v7x, 512 devices: a whole 4x8x8 slice. The times are simulated.
512 devices in a mesh: dp: 32 (over z, y_lo, core), ctx: 16 (over x, y_hi).
Axes of the slice: x: 4, y: 8 (y_hi: 4, y_lo: 2; y = y_hi * 2 + y_lo), z: 8, core: 2. Of those that a mesh axis runs over, the one named last changes fastest.
Arguments:
- queries: bfloat16 [32, 2048, 4096], P('dp', 'ctx'), may hold values from -100 to 100
- keys: bfloat16 [32, 2048, 512], P('dp', 'ctx'), may hold values from -6 to 6
- values: bfloat16 [32, 2048, 512], P('dp', 'ctx'), may hold values from -6 to 6
- out_cotangent: bfloat16 [32, 2048, 4096], P('dp', 'ctx'), may hold values from -6 to 6
- rewards: float32 [32, 6], P('dp'), may hold values from -18 to 18
- lengths: int32 [32, 6], P('dp'), may hold values from 1 to 5, 15 in all within a row
Outputs:
- attn_out: bfloat16 [32, 2048, 4096], P('dp', 'ctx')
- query_grad: bfloat16 [32, 2048, 4096], P('dp', 'ctx')
- key_grad: bfloat16 [32, 2048, 512], P('dp', 'ctx')
- value_grad: bfloat16 [32, 2048, 512], P('dp', 'ctx')
Inputs may be any that keep to these rules, and one draw needn't show every extreme that they name: Each tree's response lengths, counted in blocks of 128 tokens, sum to 15, and the longest is exactly 5 blocks.
All inputs are finite; a program needn't handle non-finite values.
Results may differ from a plain program's by a relative error of at most 0.012.
Values may be sent and summed in bfloat16 or wider, within the bound.
A program may use at most 64 MiB of HBM per device.

v0:
```python
import jax
import jax.numpy as jnp
from jax import lax
from jax.sharding import PartitionSpec as P

H = 32
KVH = 4
HD = 128
BLOCK = 128


def response_table(lengths_row, nblocks):
    block_ends = jnp.cumsum(lengths_row)
    starts = 1 + block_ends - lengths_row
    blocks = jnp.arange(nblocks, dtype=jnp.int32)
    inside = starts[None, :] <= blocks[:, None]
    first_block = jnp.max(jnp.where(inside, starts[None, :], 1), axis=1)
    return (first_block, starts)


def body(queries, keys, values, out_cotangent, rewards, lengths):
    ctx_size = lax.axis_size("ctx")
    local_tokens = queries.shape[1]
    seq_tokens = local_tokens * ctx_size
    nblocks = seq_tokens // BLOCK
    resp_count = lengths.shape[1]
    slots = max(nblocks + 1 - 2 * resp_count, 1) + 1
    local_heads = H // ctx_size
    ratio = H // KVH
    scale = HD ** (-0.5)
    group_size = 4
    group_count = nblocks // group_size
    first_block, starts = response_table(lengths[0], nblocks)
    reward_row = rewards[0]
    centered = reward_row - jnp.mean(reward_row)
    total = lax.psum(jnp.sum(centered * centered), "dp")
    advantage = centered / jnp.sqrt(total / (lax.axis_size("dp") * resp_count) + 1e-06)
    positions = lax.axis_index("ctx") * local_tokens + jnp.arange(local_tokens, dtype=jnp.int32)
    token_block = positions // BLOCK
    owner_id = jnp.sum((starts[None, :] <= token_block[:, None]).astype(jnp.int32), axis=1) - 1
    weight = jnp.sum(
        jnp.where(
            owner_id[:, None] == jnp.arange(resp_count, dtype=jnp.int32)[None, :],
            advantage[None, :],
            0.0,
        ),
        axis=1,
    )
    weighted = (weight[:, None] * out_cotangent[0].astype(jnp.float32)).astype(jnp.bfloat16)
    query_split = queries[0].reshape(local_tokens, ctx_size, local_heads * HD)
    cot_split = weighted.reshape(local_tokens, ctx_size, local_heads * HD)
    key_all, value_all = (
        lax.all_gather(keys, "ctx", axis=1, tiled=True),
        lax.all_gather(values, "ctx", axis=1, tiled=True),
    )
    head_start = lax.axis_index("ctx") * local_heads // ratio * HD
    key_rows = lax.dynamic_slice_in_dim(key_all[0], head_start, HD, 1)
    value_rows = lax.dynamic_slice_in_dim(value_all[0], head_start, HD, 1)
    key_tiles = key_rows.reshape(nblocks, BLOCK, HD)
    value_tiles = value_rows.reshape(nblocks, BLOCK, HD)
    block_ids = jnp.arange(nblocks, dtype=jnp.int32)[:, None]
    slot_ids = jnp.arange(slots, dtype=jnp.int32)[None, :]
    candidate = block_ids - (slots - 1) + slot_ids
    key_block = jnp.where(slot_ids == 0, 0, jnp.maximum(candidate, 0))
    usable = (slot_ids == 0) | (candidate >= first_block[:, None])
    causal = jnp.arange(BLOCK)[None, :] <= jnp.arange(BLOCK)[:, None]
    group_starts = jnp.arange(group_count, dtype=jnp.int32) * group_size

    def tile_scores(query_tiles, start):
        query_group = lax.dynamic_slice_in_dim(query_tiles, start, group_size, 0)
        index_rows = lax.dynamic_slice_in_dim(key_block, start, group_size, 0)
        usable_rows = lax.dynamic_slice_in_dim(usable, start, group_size, 0)
        key_group = jnp.take(key_tiles, index_rows, axis=0)
        value_group = jnp.take(value_tiles, index_rows, axis=0)
        raw = (
            jnp.einsum(
                "gihd,gmjd->ghimj", query_group, key_group, preferred_element_type=jnp.float32
            )
            * scale
        )
        query_block = start + jnp.arange(group_size, dtype=jnp.int32)
        earlier = index_rows < query_block[:, None]
        keep = usable_rows[:, None, None, :, None] & (
            earlier[:, None, None, :, None] | causal[None, None, :, None, :]
        )
        return (jnp.where(keep, raw, -jnp.inf), query_group, key_group, value_group, index_rows)

    def forward_part(scores, value_group):
        peak = jnp.max(scores, axis=(3, 4), keepdims=True)
        lse = peak + jnp.log(jnp.sum(jnp.exp(scores - peak), axis=(3, 4), keepdims=True))
        probs_low = jnp.exp(scores - lse).astype(jnp.bfloat16)
        attn = jnp.einsum(
            "ghimj,gmjd->gihd", probs_low, value_group, preferred_element_type=jnp.float32
        ).astype(jnp.bfloat16)
        return (lse, attn)

    def backward_part(scores, lse, attn, cot_group, query_group, key_group, value_group):
        probs = jnp.exp(scores - lse)
        probs_low = probs.astype(jnp.bfloat16)
        delta = jnp.sum(cot_group.astype(jnp.float32) * attn.astype(jnp.float32), axis=3)
        delta = jnp.transpose(delta, (0, 2, 1))[:, :, :, None, None]
        dprobs = jnp.einsum(
            "gihd,gmjd->ghimj", cot_group, value_group, preferred_element_type=jnp.float32
        )
        dscores = (probs * (dprobs - delta) * scale).astype(jnp.bfloat16)
        qgrad = jnp.einsum(
            "ghimj,gmjd->gihd", dscores, key_group, preferred_element_type=jnp.float32
        ).astype(jnp.bfloat16)
        key_part = jnp.einsum(
            "ghimj,gihd->gmjd", dscores, query_group, preferred_element_type=jnp.float32
        )
        value_part = jnp.einsum(
            "ghimj,gihd->gmjd", probs_low, cot_group, preferred_element_type=jnp.float32
        )
        return (qgrad, key_part, value_part)

    empty = jnp.zeros((nblocks, BLOCK, HD), jnp.float32)
    query_cols = lax.all_to_all(query_split, "ctx", split_axis=1, concat_axis=0, tiled=True)
    query_tiles = query_cols.reshape(nblocks, BLOCK, local_heads, HD)

    def forward_step(start):
        scores, query_group, key_group, value_group, index_rows = tile_scores(query_tiles, start)
        return forward_part(scores, value_group)

    lse_all, attn_all = lax.map(forward_step, group_starts)
    cot_cols = lax.all_to_all(cot_split, "ctx", split_axis=1, concat_axis=0, tiled=True)
    cot_tiles = cot_cols.reshape(nblocks, BLOCK, local_heads, HD)

    def backward_step(carry, inputs):
        start, lse, attn = inputs
        scores, query_group, key_group, value_group, index_rows = tile_scores(query_tiles, start)
        cot_group = lax.dynamic_slice_in_dim(cot_tiles, start, group_size, 0)
        qgrad, key_part, value_part = backward_part(
            scores, lse, attn, cot_group, query_group, key_group, value_group
        )
        return (
            (carry[0].at[index_rows].add(key_part), carry[1].at[index_rows].add(value_part)),
            qgrad,
        )

    (key_acc, value_acc), qgrad_all = lax.scan(
        backward_step, (empty, empty), (group_starts, lse_all, attn_all)
    )
    attn_heads = attn_all.reshape(seq_tokens, 1, local_heads * HD)
    qgrad_heads = qgrad_all.reshape(seq_tokens, 1, local_heads * HD)
    attn_back, qgrad_back = (
        lax.all_to_all(attn_heads, "ctx", split_axis=0, concat_axis=1, tiled=True),
        lax.all_to_all(qgrad_heads, "ctx", split_axis=0, concat_axis=1, tiled=True),
    )
    key_back, value_back = (
        lax.all_to_all(
            key_acc.reshape(seq_tokens, 1, HD).astype(jnp.bfloat16),
            "ctx",
            split_axis=0,
            concat_axis=1,
            tiled=True,
        ).astype(jnp.float32),
        lax.all_to_all(
            value_acc.reshape(seq_tokens, 1, HD).astype(jnp.bfloat16),
            "ctx",
            split_axis=0,
            concat_axis=1,
            tiled=True,
        ).astype(jnp.float32),
    )
    key_sum = jnp.sum(key_back.reshape(local_tokens, KVH, ctx_size // KVH, HD), axis=2)
    value_sum = jnp.sum(value_back.reshape(local_tokens, KVH, ctx_size // KVH, HD), axis=2)
    attn_out = attn_back.reshape(1, local_tokens, H * HD)
    query_grad = qgrad_back.reshape(1, local_tokens, H * HD)
    key_grad = key_sum.reshape(1, local_tokens, KVH * HD).astype(jnp.bfloat16)
    value_grad = value_sum.reshape(1, local_tokens, KVH * HD).astype(jnp.bfloat16)
    return (attn_out, query_grad, key_grad, value_grad)


def solution(mesh):
    placed = (
        P("dp", "ctx", None),
        P("dp", "ctx", None),
        P("dp", "ctx", None),
        P("dp", "ctx", None),
        P("dp", None),
        P("dp", None),
    )
    return jax.shard_map(
        body,
        mesh=mesh,
        in_specs=placed,
        out_specs=(
            P("dp", "ctx", None),
            P("dp", "ctx", None),
            P("dp", "ctx", None),
            P("dp", "ctx", None),
        ),
        check_vma=False,
    )
```

profile of v0, /device:TPU:64, one launch (start us, length us, event | category | flops | bytes accessed | tf_op | source)
XLA Modules:
  0.0 496.8 jit_solution(16300572905384726460)
XLA Ops:
  14.2 9.7 %all-to-all-start = ((bf16[128,16,256]{0,2,1:T(8,128)(2,1)}), bf16[128,16,256]{0,2,1:T(8,128)(2,1)S(1)}, u32[]{:S(2)}, u32[]{:S(2)}) async-start(bf16[128,16,256]{0,2,1:T(8,128)(2,1)} %bitcast.2), calls=%async_computation | async-start | bytes 2097152 | tf_op jit(solution)/shard_map/all_to_all | solution.py:118
  23.8 72.0 %psum.7 = f32[]{:T(128)} all-reduce(f32[]{:T(128)} %multiply_reduce_fusion), channel_id=1, replica_groups=mesh['dp'=32,'ctx'=16] {'dp'}, use_global_device_ids=true, to_apply=%region_9.11 | all-reduce | flops 1 | bytes 8 | tf_op jit(solution)/shard_map/psum | solution.py:36
  100.0 15.2 %all-to-all-start.2 = ((bf16[128,16,256]{0,2,1:T(8,128)(2,1)}), bf16[128,16,256]{0,2,1:T(8,128)(2,1)}, u32[]{:S(2)}, u32[]{:S(2)}) async-start(bf16[128,16,256]{0,2,1:T(8,128)(2,1)} %multiply_convert_fusion), calls=%async_computation.2 | async-start | bytes 2097152 | tf_op jit(solution)/shard_map/all_to_all | solution.py:126
  117.6 58.7 %all-gather.5.cloned.1.call-done = bf16[1,2048,512]{2,1,0:T(8,128)(2,1)} async-done(((bf16[1,128,512]{2,1,0:T(8,128)(2,1)}), bf16[1,2048,512]{2,1,0:T(8,128)(2,1)}) %all-gather.5.cloned.1.call-update) | async-done | bytes 2097168 | tf_op jit(solution)/shard_map/all_gather | solution.py:54
  177.3 52.9 %while.28 = (s32[]{:T(128)}, f32[4,4,2,128,1,1]{3,2,1,5,4,0:T(2,128)S(1)}, bf16[4,4,128,2,128]{2,4,3,1,0:T(8,128)(2,1)}, s32[4]{0:T(128)S(1)}, pred[16,6]{1,0:T(...) while((s32[]{:T(128)}, ...), condition=%wide.region_5.7_spmd.clone, body=%wide.region_2.0_spmd.clone.sunk | while | flops 413024448 | bytes 30479952 | solution.py:125
  232.4 144.0 %while.29 = (s32[]{:T(128)}, f32[16,128,128]{2,1,0:T(8,128)}, f32[16,128,128]{2,1,0:T(8,128)}, bf16[4,4,128,2,128]{4,3,2,1,0:T(2,128)(2,1)}, s32[4]{0:T(128)S(1)...) while((s32[]{:T(128)}, f32[16,128,128]{2,1,0:T(8,128)}, ...), condition=%wide.region_15.17_spmd.clone, body=%wide.region_11.16_spmd.clone.sunk | while | flops 1018708160 | bytes 54720396 | solution.py:141
  236.8 3.6 fusion.105
  252.9 6.5 %scatter_fusion = f32[16,128,128]{2,1,0:T(8,128)} fusion(f32[16,128,128]{2,1,0:T(8,128)} %get-tuple-element.591, s32[24]{0:T(128)S(1)} %reshape.377, f32[24,128,128]{2,1,0:T(8,128)S(1)} %bitcast.252), kind=kCustom, calls=%fused_computation.4.clone.clone.1 | custom fusion | flops 393216 | bytes 4718688 | tf_op jit(solution)/shard_map/while/body/eval_jaxpr/scatter-add | solution.py:137
  259.4 3.9 fusion.109
  263.3 4.5 scatter_fusion.1
  289.4 6.0 %scatter_fusion = f32[16,128,128]{2,1,0:T(8,128)} fusion(f32[16,128,128]{2,1,0:T(8,128)} %get-tuple-element.591, s32[24]{0:T(128)S(1)} %reshape.377, f32[24,128,128]{2,1,0:T(8,128)S(1)} %bitcast.252), kind=kCustom, calls=%fused_computation.4.clone.clone.1 | custom fusion | flops 393216 | bytes 4718688 | tf_op jit(solution)/shard_map/while/body/eval_jaxpr/scatter-add | solution.py:137
  295.3 3.9 fusion.109
  299.3 4.5 scatter_fusion.1
  309.2 3.6 fusion.105
  325.3 5.9 %scatter_fusion = f32[16,128,128]{2,1,0:T(8,128)} fusion(f32[16,128,128]{2,1,0:T(8,128)} %get-tuple-element.591, s32[24]{0:T(128)S(1)} %reshape.377, f32[24,128,128]{2,1,0:T(8,128)S(1)} %bitcast.252), kind=kCustom, calls=%fused_computation.4.clone.clone.1 | custom fusion | flops 393216 | bytes 4718688 | tf_op jit(solution)/shard_map/while/body/eval_jaxpr/scatter-add | solution.py:137
  331.2 3.9 fusion.109
  335.1 4.5 scatter_fusion.1
  345.0 3.6 fusion.105
  361.1 5.9 %scatter_fusion = f32[16,128,128]{2,1,0:T(8,128)} fusion(f32[16,128,128]{2,1,0:T(8,128)} %get-tuple-element.591, s32[24]{0:T(128)S(1)} %reshape.377, f32[24,128,128]{2,1,0:T(8,128)S(1)} %bitcast.252), kind=kCustom, calls=%fused_computation.4.clone.clone.1 | custom fusion | flops 393216 | bytes 4718688 | tf_op jit(solution)/shard_map/while/body/eval_jaxpr/scatter-add | solution.py:137
  367.0 3.9 fusion.109
  371.0 4.5 scatter_fusion.1
  380.3 6.0 %all-to-all-start.4 = ((bf16[16,2,8192]{2,1,0:T(2,128)(2,1)}), bf16[16,2,8192]{2,1,0:T(2,128)(2,1)S(1)}, u32[]{:S(2)}, u32[]{:S(2)}) async-start(bf16[16,2,8192]{2,1,0:T(2,128)(2,1)} %reshape.346), calls=%async_computation.4 | async-start | bytes 1048576 | tf_op jit(solution)/shard_map/all_to_all | solution.py:151
  388.3 16.1 %all-to-all-done.4 = bf16[16,2,8192]{2,1,0:T(2,128)(2,1)S(1)} async-done(((bf16[16,2,8192]{2,1,0:T(2,128)(2,1)}), bf16[16,2,8192]{2,1,0:T(2,128)(2,1)S(1)}, u32[]{:S(2)}, u32[]{:S(2)}) %all-to-all-start.4) | async-done | bytes 524320 | tf_op jit(solution)/shard_map/all_to_all | solution.py:151
  404.5 4.2 all-to-all-start.5
  409.2 11.7 %reduce.5 = bf16[2048,256]{1,0:T(8,128)(2,1)} reduce(bf16[2048,1,256]{2,1,0:T(2,128)(2,1)S(1)} %reshape.341, bf16[]{:T(256)} %broadcast.254), dimensions={1}, to_apply=%reshape.341.reduce_sub_computation | reduce | bytes 2097154 | tf_op jit(solution)/shard_map/reshape | solution.py:145
  424.7 7.9 %all-to-all-start.3 = ((bf16[16,2,16384]{2,1,0:T(2,128)(2,1)}), bf16[16,2,16384]{2,1,0:T(2,128)(2,1)}, u32[]{:S(2)}, u32[]{:S(2)}) async-start(bf16[16,2,16384]{2,1,0:T(2,128)(2,1)} %reshape.344), calls=%async_computation.3 | async-start | bytes 2097152 | tf_op jit(solution)/shard_map/all_to_all | solution.py:148
  434.7 6.4 %reshape.340 = bf16[2048,1,256]{2,1,0:T(2,128)(2,1)S(1)} reshape(bf16[4,4,128,2,128]{4,3,2,1,0:T(2,128)(2,1)} %copy.97) | data formatting | bytes 2097152 | tf_op jit(solution)/shard_map/reshape | solution.py:144
  441.0 10.6 %reduce.4 = bf16[2048,256]{1,0:T(8,128)(2,1)S(1)} reduce(bf16[2048,1,256]{2,1,0:T(2,128)(2,1)S(1)} %reshape.340, bf16[]{:T(256)} %broadcast.254), dimensions={1}, to_apply=%reshape.340.reduce_sub_computation | reduce | bytes 2097154 | tf_op jit(solution)/shard_map/reshape | solution.py:144
  452.7 4.7 all-to-all-done.3
  457.5 4.8 all-to-all-start.1
  467.3 4.3 reshape.345
  475.7 11.1 %all-to-all-done.1 = bf16[16,2,16384]{2,1,0:T(2,128)(2,1)S(1)} async-done(((bf16[16,2,16384]{2,1,0:T(2,128)(2,1)}), bf16[16,2,16384]{2,1,0:T(2,128)(2,1)S(1)}, u32[]{:S(2)}, u32[]{:S(2)}) %all-to-all-start.1) | async-done | bytes 1048608 | tf_op jit(solution)/shard_map/all_to_all | solution.py:147
  (249 shorter events, 152.7 us)
Async XLA Ops:
  7.2 88.7 %copy-start.10 = (s32[1,6]{1,0:T(1,128)S(1)}, s32[1,6]{1,0:T(1,128)}, u32[]{:S(2)}) copy-start(s32[1,6]{1,0:T(1,128)} %param.17) | copy-start | bytes 76
  7.2 109.3 %all-gather.3.cloned.1.call-start = ((), (), s32[]{:S(2)}) async-start(), calls=%async_computation.6 | async-start | bytes 2228224 | tf_op jit(solution)/shard_map/all_gather | solution.py:53
  7.9 168.4 %all-gather.5.cloned.1.call-start = ((), (), s32[]{:S(2)}) async-start(), calls=%async_computation.7 | async-start | bytes 2228224 | tf_op jit(solution)/shard_map/all_gather | solution.py:54
  10.9 87.6 %copy-start.9 = (f32[1,6]{1,0:T(1,128)S(1)}, f32[1,6]{1,0:T(1,128)}, u32[]{:S(2)}) copy-start(f32[1,6]{1,0:T(1,128)} %param.16) | copy-start | bytes 76
  14.2 85.8 %all-to-all-start = ((bf16[128,16,256]{0,2,1:T(8,128)(2,1)}), bf16[128,16,256]{0,2,1:T(8,128)(2,1)S(1)}, u32[]{:S(2)}, u32[]{:S(2)}) async-start(bf16[128,16,256]{0,2,1:T(8,128)(2,1)} %bitcast.2), calls=%async_computation | async-start | bytes 2097152 | tf_op jit(solution)/shard_map/all_to_all | solution.py:118
  100.0 130.2 %all-to-all-start.2 = ((bf16[128,16,256]{0,2,1:T(8,128)(2,1)}), bf16[128,16,256]{0,2,1:T(8,128)(2,1)}, u32[]{:S(2)}, u32[]{:S(2)}) async-start(bf16[128,16,256]{0,2,1:T(8,128)(2,1)} %multiply_convert_fusion), calls=%async_computation.2 | async-start | bytes 2097152 | tf_op jit(solution)/shard_map/all_to_all | solution.py:126
  183.5 1.7 copy-start.3
  196.7 1.7 copy-start.3
  209.9 1.7 copy-start.3
  223.1 1.7 copy-start.3
  248.3 1.1 copy-start.4
  259.4 3.9 copy-start
  267.8 1.0 copy-start.1
  284.7 1.1 copy-start.4
  295.3 3.9 copy-start
  303.8 1.0 copy-start.1
  320.7 1.1 copy-start.4
  331.2 3.9 copy-start
  339.6 1.0 copy-start.1
  356.5 1.1 copy-start.4
  367.0 3.9 copy-start
  375.4 1.0 copy-start.1
  376.4 9.9 %copy-start.2 = (f32[16,128,128]{2,1,0:T(8,128)S(1)}, f32[16,128,128]{2,1,0:T(8,128)}, u32[]{:S(2)}) copy-start(f32[16,128,128]{2,1,0:T(8,128)} %get-tuple-element.136) | copy-start | bytes 3145732
  380.3 28.4 %copy-start.8 = (bf16[4,4,128,2,128]{4,3,2,1,0:T(2,128)(2,1)S(1)}, bf16[4,4,128,2,128]{4,3,2,1,0:T(2,128)(2,1)}, u32[]{:S(2)}) copy-start(bf16[4,4,128,2,128]{4,3,2,1,0:T(2,128)(2,1)} %get-tuple-element.134) | copy-start | bytes 3145732
  380.3 24.2 %all-to-all-start.4 = ((bf16[16,2,8192]{2,1,0:T(2,128)(2,1)}), bf16[16,2,8192]{2,1,0:T(2,128)(2,1)S(1)}, u32[]{:S(2)}, u32[]{:S(2)}) async-start(bf16[16,2,8192]{2,1,0:T(2,128)(2,1)} %reshape.346), calls=%async_computation.4 | async-start | bytes 1048576 | tf_op jit(solution)/shard_map/all_to_all | solution.py:151
  404.5 4.2 copy-start.6
  404.5 20.3 %all-to-all-start.5 = ((bf16[16,2,8192]{2,1,0:T(2,128)(2,1)}), bf16[16,2,8192]{2,1,0:T(2,128)(2,1)}, u32[]{:S(2)}, u32[]{:S(2)}) async-start(bf16[16,2,8192]{2,1,0:T(2,128)(2,1)} %reshape.348), calls=%async_computation.5 | async-start | bytes 1048576 | tf_op jit(solution)/shard_map/all_to_all | solution.py:158
  409.2 23.4 %copy-start.5 = (bf16[4,4,128,2,128]{2,4,3,1,0:T(8,128)(2,1)S(1)}, bf16[4,4,128,2,128]{2,4,3,1,0:T(8,128)(2,1)}, u32[]{:S(2)}) copy-start(bf16[4,4,128,2,128]{2,4,3,1,0:T(8,128)(2,1)} %get-tuple-element.626) | copy-start | bytes 3145732
  424.7 32.8 %all-to-all-start.3 = ((bf16[16,2,16384]{2,1,0:T(2,128)(2,1)}), bf16[16,2,16384]{2,1,0:T(2,128)(2,1)}, u32[]{:S(2)}, u32[]{:S(2)}) async-start(bf16[16,2,16384]{2,1,0:T(2,128)(2,1)} %reshape.344), calls=%async_computation.3 | async-start | bytes 2097152 | tf_op jit(solution)/shard_map/all_to_all | solution.py:148
  451.6 10.7 %copy-start.7 = (bf16[16,2,8192]{2,1,0:T(2,128)(2,1)S(1)}, bf16[16,2,8192]{2,1,0:T(2,128)(2,1)}, u32[]{:S(2)}) copy-start(bf16[16,2,8192]{2,1,0:T(2,128)(2,1)} %copy-done.6) | copy-start | bytes 1572868
  457.5 29.3 %all-to-all-start.1 = ((bf16[16,2,16384]{2,1,0:T(2,128)(2,1)}), bf16[16,2,16384]{2,1,0:T(2,128)(2,1)S(1)}, u32[]{:S(2)}, u32[]{:S(2)}) async-start(bf16[16,2,16384]{2,1,0:T(2,128)(2,1)} %reshape.342), calls=%async_computation.1 | async-start | bytes 2097152 | tf_op jit(solution)/shard_map/all_to_all | solution.py:147
Sparse Core Ops, SparseCore 0:
  11.0 82.9 all-gather.2
  97.0 79.2 all-gather.4
where the time goes:
time: 500 us; the launch traced here: 497 us
  waiting for transfers between devices  93.6 us (19%)
  local copies, waits for them, and re-layouts  91.7 us (18%)
  other arithmetic  85.3 us (17%)
  matrix products  74.2 us (15%)
  blocking collectives  72 us (14%)
  starting transfers between devices  47.9 us (10%)
  loops' own time  16.3 us (3%)
  between operations  15.7 us (3%)
    psum x1, blocking collectives, body(): total = lax.psum(jnp.sum(centered * centered), 'dp')  72 us
    all_gather x1, waiting for transfers between devices, body(): lax.all_gather(values, 'ctx', axis=1, tiled=True)  58.7 us
    scatter-add x4, other arithmetic, backward_step(): carry[0].at[index_rows].add(key_part)  24.2 us
    unnamed x32, local copies, waits for them, and re-layouts  22.5 us
    dot_general x8, matrix products, tile_scores(): jnp.einsum('gihd,gmjd->ghimj', query_group, key_group, preferred_element_...  21.1 us
    scatter-add x4, other arithmetic, backward_step(): carry[1].at[index_rows].add(value_part)  17.9 us
    all_to_all x1, waiting for transfers between devices, body(): lax.all_to_all(key_acc.reshape(seq_tokens, 1, HD).astype(jnp.bfloat16), '...  16.1 us
    dot_general x4, matrix products, backward_part(): jnp.einsum('ghimj,gihd->gmjd', probs_low, cot_group, preferred_element_ty...  15.7 us
  transfers between devices with their start and end apart: 8, of which 5 were waited for; matrix products, arithmetic and copies ran while one was open for 20% of the time, Pallas kernels for 0%

commit v1 on v0

v1 whole, which is shorter than its diff:
```python
import functools

import jax
import jax.numpy as jnp
from jax import lax
from jax.experimental import pallas as pl
from jax.experimental.pallas import tpu as pltpu
from jax.sharding import PartitionSpec as P

H = 32
KVH = 4
HD = 128
BLOCK = 128
RESP = 6
BACK = 4
SLOTS = BACK + 2
OWN = SLOTS - 1
COLS = 4
QUAD = 4
RATIO = H // KVH
PAIRS = RATIO // 2
WIDE = 2 * BLOCK
SCALE = HD ** (-0.5)
LOG2E = 1.4426950408889634
MASKED = -1e30
MESH = pl.DeviceIdType.MESH
NT = (((1,), (1,)), ((), ()))
NN = (((1,), (0,)), ((), ()))


def dot(a, b, dims=NN):
    return lax.dot_general(a, b, dims, preferred_element_type=jnp.float32)


def kernel(
    ctx,
    dp,
    q_ref,
    c_ref,
    k_ref,
    v_ref,
    rew_ref,
    len_ref,
    o_ref,
    dq_ref,
    dk_ref,
    dv_ref,
    kv,
    kt,
    vt,
    acc,
    own,
    give,
    got,
    chain,
    stat,
    quad_got,
    line_got,
    fsend,
    frecv,
    rsend,
    gsend,
    grecv,
    csend,
    crecv,
    qsend,
    qrecv,
    lsend,
    lrecv,
):
    me = lax.axis_index("ctx")
    col = me // COLS
    last = ctx // COLS - 1
    my_dp = lax.axis_index("dp")
    quads = dp // QUAD

    barrier = pltpu.get_barrier_semaphore()

    def greet_ctx(d, carry):
        pl.semaphore_signal(
            barrier, inc=1, device_id={"ctx": lax.rem(me + d, ctx)}, device_id_type=MESH
        )
        return carry

    lax.fori_loop(1, ctx, greet_ctx, 0)
    greeted = ctx - 1
    quad_base = my_dp // QUAD * QUAD
    quad_at = my_dp - quad_base

    def quad_peer(d):
        return quad_base + lax.rem(quad_at + d, QUAD)

    def line_peer(d):
        return lax.rem(my_dp // QUAD + d, quads) * QUAD + quad_at

    if dp > 1:
        for d in range(1, QUAD):
            pl.semaphore_signal(barrier, inc=1, device_id={"dp": quad_peer(d)}, device_id_type=MESH)
        for d in range(1, quads):
            pl.semaphore_signal(barrier, inc=1, device_id={"dp": line_peer(d)}, device_id_type=MESH)
        greeted += QUAD - 1 + quads - 1

    for g in range(KVH):
        kv[g, OWN, 0] = k_ref[:, g * HD : (g + 1) * HD]
        kv[g, OWN, 1] = v_ref[:, g * HD : (g + 1) * HD]

    def blank(slot):
        for g in range(KVH):
            kv[g, slot] = jnp.zeros((2, BLOCK, HD), jnp.bfloat16)

    @pl.when(me == 0)
    def _():
        blank(0)

    for k in range(1, BACK + 1):

        @pl.when(me <= k)
        def _():
            blank(OWN - k)

    mean = rew_ref[0, 0]
    for r in range(1, RESP):
        mean = mean + rew_ref[0, r]
    mean = mean * (1.0 / RESP)
    square = jnp.float32(0.0)
    advantage = jnp.float32(0.0)
    first = jnp.int32(1)
    start = jnp.int32(1)
    for r in range(RESP):
        centered = rew_ref[0, r] - mean
        square = square + centered * centered
        advantage = jnp.where(start <= me, centered, advantage)
        first = jnp.where(start <= me, start, first)
        start = start + len_ref[0, r]
    stat[0] = jnp.full((8, HD), square, jnp.float32)
    bias = [jnp.where(me >= 1, 0.0, MASKED).astype(jnp.float32)]
    for k in range(BACK, 0, -1):
        bias.append(jnp.where(me - k >= first, 0.0, MASKED).astype(jnp.float32))

    pl.semaphore_wait(barrier, greeted)

    def key_copy(g, src_slot, dst_slot, send, target):
        return pltpu.make_async_remote_copy(
            src_ref=kv.at[g, src_slot],
            dst_ref=kv.at[g, dst_slot],
            send_sem=send,
            recv_sem=frecv.at[g, dst_slot],
            device_id={"ctx": target},
            device_id_type=MESH,
        )

    sends = [((me >= 1) & (me + k < ctx), k, OWN - k) for k in range(1, BACK + 1)]
    sends += [(me == 0, k, 0) for k in (1, 2, 3, COLS, last * COLS)]

    def each_send(g, do):
        for n, (when, distance, slot) in enumerate(sends):

            @pl.when(when)
            def _():
                do(key_copy(g, OWN, slot, fsend.at[g, n], lax.rem(me + distance, ctx)))

    def send_group(g, carry):
        each_send(g, lambda copy: copy.start())
        return carry

    lax.fori_loop(0, KVH, send_group, 0)

    relays = [
        ((me >= 1) & (me < 2 * COLS), COLS),
        ((me >= 1) & (me < COLS), last * COLS),
    ]

    def each_relay(g, do):
        for n, (when, distance) in enumerate(relays):
            if n == 0:
                when = when & (me + COLS < last * COLS)

            @pl.when(when)
            def _():
                do(key_copy(g, 0, 0, rsend.at[g, n], lax.rem(me + distance, ctx)))

    def take_prompt(g):
        @pl.when(me >= 1)
        def _():
            key_copy(g, OWN, 0, fsend.at[g, 0], lax.rem(me + 1, ctx)).wait_recv()

        each_relay(g, lambda copy: copy.start())

    def share(src, dst, send, recv, target):
        return pltpu.make_async_remote_copy(
            src_ref=src,
            dst_ref=dst,
            send_sem=send,
            recv_sem=recv,
            device_id={"dp": target},
            device_id_type=MESH,
        )

    def quad_copy(d):
        return share(
            stat.at[0], quad_got.at[d - 1], qsend.at[d - 1], qrecv.at[d - 1], quad_peer(d)
        )

    def line_copy(d):
        return share(
            stat.at[1], line_got.at[d - 1], lsend.at[d - 1], lrecv.at[d - 1], line_peer(d)
        )

    if dp > 1:
        for d in range(1, QUAD):
            quad_copy(d).start()
        for d in range(1, QUAD):
            quad_copy(d).wait()
        part = stat[0]
        for d in range(1, QUAD):
            part = part + quad_got[d - 1]
        stat[1] = part
        for d in range(1, quads):
            line_copy(d).start()
    take_prompt(0)
    if dp > 1:
        for d in range(1, quads):
            line_copy(d).wait()
        total = stat[1]
        for d in range(1, quads):
            total = total + line_got[d - 1]
    else:
        total = stat[0]
    weight = advantage * SCALE / jnp.sqrt(total * (1.0 / (dp * RESP)) + 1e-06)
    stat[0] = weight

    def grad_copy(g, k):
        return pltpu.make_async_remote_copy(
            src_ref=give.at[g, OWN - k],
            dst_ref=got.at[g, k - 1],
            send_sem=gsend.at[g, k - 1],
            recv_sem=grecv.at[g, k - 1],
            device_id={"ctx": lax.rem(me + ctx - k, ctx)},
            device_id_type=MESH,
        )

    def each_grad(g, do):
        for k in range(1, BACK + 1):

            @pl.when(me > k)
            def _():
                do(grad_copy(g, k))

    def chain_copy(g, n, distance):
        return pltpu.make_async_remote_copy(
            src_ref=give.at[g, 0],
            dst_ref=chain.at[g, n],
            send_sem=csend.at[g],
            recv_sem=crecv.at[g, n],
            device_id={"ctx": lax.rem(me + ctx - distance, ctx)},
            device_id_type=MESH,
        )

    def home_copy(g, k):
        return pltpu.make_async_remote_copy(
            src_ref=give.at[g, 0],
            dst_ref=got.at[g, k - 1],
            send_sem=csend.at[g],
            recv_sem=grecv.at[g, k - 1],
            device_id={"ctx": lax.rem(me + ctx - k, ctx)},
            device_id_type=MESH,
        )

    in_first = (me >= 1) & (me < COLS)
    in_second = (me >= COLS) & (me < 2 * COLS)
    in_third = (me >= 2 * COLS) & (me < last * COLS)
    in_last = me >= last * COLS

    def chain_ends(g, do):
        @pl.when(in_third)
        def _():
            do(chain_copy(g, 0, COLS))

        @pl.when(in_last)
        def _():
            do(chain_copy(g, 1, last * COLS))

    def chain_middle(g):
        @pl.when(in_second)
        def _():
            chain_copy(g, 0, COLS).wait_recv()
            give[g, 0] = (
                give[g, 0].astype(jnp.float32) + chain[g, 0].astype(jnp.float32)
            ).astype(jnp.bfloat16)
            chain_copy(g, 0, COLS).start()

    def chain_home(g):
        @pl.when(in_first)
        def _():
            chain_copy(g, 0, COLS).wait_recv()
            chain_copy(g, 1, COLS).wait_recv()
            give[g, 0] = (
                give[g, 0].astype(jnp.float32)
                + chain[g, 0].astype(jnp.float32)
                + chain[g, 1].astype(jnp.float32)
            ).astype(jnp.bfloat16)
            for k in range(1, COLS):

                @pl.when(me == k)
                def _():
                    home_copy(g, k).start()

    row = lax.broadcasted_iota(jnp.int32, (BLOCK, WIDE), 0)
    column = lax.broadcasted_iota(jnp.int32, (BLOCK, WIDE), 1)
    causal = row <= lax.rem(column, BLOCK)

    def pair_step(g, pair):
        base = pl.multiple_of(g * (RATIO * HD) + pair * WIDE, WIDE)
        left = pl.ds(base, HD)
        right = pl.ds(pl.multiple_of(base + HD, HD), HD)
        query = jnp.concatenate([q_ref[:, left], q_ref[:, right]], axis=0)
        cot = jnp.concatenate([c_ref[:, left], c_ref[:, right]], axis=0)
        keys = kv[g, :, 0].reshape(SLOTS * BLOCK, HD)
        values = kv[g, :, 1].reshape(SLOTS * BLOCK, HD)
        raw = dot(keys, query, NT) * (SCALE * LOG2E)
        tiles = [raw[s * BLOCK : (s + 1) * BLOCK] + bias[s] for s in range(OWN)]
        tiles.append(jnp.where(causal, raw[OWN * BLOCK :], MASKED))
        scores = jnp.concatenate(tiles, axis=0)
        peak = jnp.max(scores, axis=0, keepdims=True)
        exps = jnp.exp2(scores - peak)
        probs = exps * (1.0 / jnp.sum(exps, axis=0, keepdims=True))
        low = probs.astype(jnp.bfloat16)
        dprobs = dot(values, cot, NT)
        delta = jnp.sum(probs * dprobs, axis=0, keepdims=True)
        dscores = (probs * (dprobs - delta)).astype(jnp.bfloat16)
        attn = dot(vt[...], low)
        qgrad = dot(kt[...], dscores) * stat[0, 0:1, 0:1]
        acc[0] += dot(dscores, query)
        acc[1] += dot(low, cot)
        o_ref[:, left] = attn[:, :HD].T.astype(jnp.bfloat16)
        o_ref[:, right] = attn[:, HD:].T.astype(jnp.bfloat16)
        dq_ref[:, left] = qgrad[:, :HD].T.astype(jnp.bfloat16)
        dq_ref[:, right] = qgrad[:, HD:].T.astype(jnp.bfloat16)

    def group_step(g, carry):
        for k in range(1, BACK + 1):

            @pl.when(me > k)
            def _():
                key_copy(g, OWN, OWN - k, fsend.at[g, 0], lax.rem(me + 1, ctx)).wait_recv()

        kt[...] = kv[g, :, 0].reshape(SLOTS * BLOCK, HD).T
        vt[...] = kv[g, :, 1].reshape(SLOTS * BLOCK, HD).T
        acc[...] = jnp.zeros_like(acc)

        def pairs(pair, inner):
            pair_step(g, pair)
            return inner

        lax.fori_loop(0, PAIRS // 2, pairs, 0)

        @pl.when(g < KVH - 1)
        def _():
            take_prompt(g + 1)

        @pl.when(g > 0)
        def _():
            chain_middle(g - 1)

        lax.fori_loop(PAIRS // 2, PAIRS, pairs, 0)

        scale = stat[0, 0:1, :]
        for s in range(OWN):
            rows = pl.ds(s * BLOCK, BLOCK)
            give[g, s, 0] = (acc[0, rows, :] * scale).astype(jnp.bfloat16)
            give[g, s, 1] = (acc[1, rows, :] * (scale * (1.0 / SCALE))).astype(jnp.bfloat16)
        rows = pl.ds(OWN * BLOCK, BLOCK)
        own[g, 0] = acc[0, rows, :] * scale
        own[g, 1] = acc[1, rows, :] * (scale * (1.0 / SCALE))
        each_grad(g, lambda copy: copy.start())
        chain_ends(g, lambda copy: copy.start())

        @pl.when(g > 0)
        def _():
            chain_home(g - 1)

        return carry

    lax.fori_loop(0, KVH, group_step, 0)
    chain_middle(KVH - 1)
    chain_home(KVH - 1)

    def close_group(g, carry):
        def add(part):
            own[g] += part.astype(jnp.float32)

        for k in range(1, BACK + 1):
            here = (me >= 1) & (me + k < ctx)
            if k < COLS:
                here = here | (me == 0)

            @pl.when(here)
            def _():
                grad_copy(g, k).wait_recv()
                add(got[g, k - 1])

        @pl.when(me == 0)
        def _():
            for n in range(2):
                chain_copy(g, n, COLS).wait_recv()
                add(chain[g, n])

        at = pl.ds(pl.multiple_of(g * HD, HD), HD)
        dk_ref[:, at] = own[g, 0].astype(jnp.bfloat16)
        dv_ref[:, at] = own[g, 1].astype(jnp.bfloat16)
        return carry

    lax.fori_loop(0, KVH, close_group, 0)

    def settle(g, carry):
        each_send(g, lambda copy: copy.wait_send())
        each_relay(g, lambda copy: copy.wait_send())
        each_grad(g, lambda copy: copy.wait_send())

        @pl.when(me >= 1)
        def _():
            chain_copy(g, 0, COLS).wait_send()

        return carry

    lax.fori_loop(0, KVH, settle, 0)


def body(queries, keys, values, out_cotangent, rewards, lengths):
    ctx = lax.axis_size("ctx")
    dp = lax.axis_size("dp")
    tokens = queries.shape[1]
    vmem = pl.BlockSpec(memory_space=pltpu.VMEM)
    smem = pl.BlockSpec(memory_space=pltpu.SMEM)
    wide = jax.ShapeDtypeStruct((tokens, H * HD), jnp.bfloat16)
    thin = jax.ShapeDtypeStruct((tokens, KVH * HD), jnp.bfloat16)
    block = (2, BLOCK, HD)
    quads = max(dp // QUAD - 1, 1)
    dma = pltpu.SemaphoreType.DMA
    outs = pl.pallas_call(
        functools.partial(kernel, ctx, dp),
        out_shape=(wide, wide, thin, thin),
        in_specs=[vmem] * 4 + [smem] * 2,
        out_specs=(vmem,) * 4,
        scratch_shapes=[
            pltpu.VMEM((KVH, SLOTS) + block, jnp.bfloat16),
            pltpu.VMEM((HD, SLOTS * BLOCK), jnp.bfloat16),
            pltpu.VMEM((HD, SLOTS * BLOCK), jnp.bfloat16),
            pltpu.VMEM((2, SLOTS * BLOCK, HD), jnp.float32),
            pltpu.VMEM((KVH,) + block, jnp.float32),
            pltpu.VMEM((KVH, OWN) + block, jnp.bfloat16),
            pltpu.VMEM((KVH, BACK) + block, jnp.bfloat16),
            pltpu.VMEM((KVH, 2) + block, jnp.bfloat16),
            pltpu.VMEM((2, 8, HD), jnp.float32),
            pltpu.VMEM((QUAD - 1, 8, HD), jnp.float32),
            pltpu.VMEM((quads, 8, HD), jnp.float32),
            dma((KVH, BACK + 5)),
            dma((KVH, SLOTS)),
            dma((KVH, 2)),
            dma((KVH, BACK)),
            dma((KVH, BACK)),
            dma((KVH,)),
            dma((KVH, 2)),
            dma((QUAD - 1,)),
            dma((QUAD - 1,)),
            dma((quads,)),
            dma((quads,)),
        ],
        compiler_params=pltpu.CompilerParams(
            collective_id=0, has_side_effects=True, vmem_limit_bytes=48 * 1024 * 1024
        ),
        name="tree_attention",
    )(queries[0], out_cotangent[0], keys[0], values[0], rewards, lengths)
    return tuple(out[None] for out in outs)


def solution(mesh):
    placed = (P("dp", "ctx", None),) * 4
    return jax.shard_map(
        body,
        mesh=mesh,
        in_specs=placed + (P("dp", None),) * 2,
        out_specs=placed,
        check_vma=False,
    )
```

time: 500 us -> 109 us (0.22)
  the two profiles are of different devices: /device:TPU:64 before, /device:TPU:8 now
where the time goes in v1:
time: 109 us; the launch traced here: 108 us
  Pallas kernels  99.6 us (91%)
  local copies, waits for them, and re-layouts  8.16 us (7%)
    pallas_call x1, Pallas kernels, body(): pl.pallas_call(functools.partial(kernel, ctx, dp), out_shape=(wide, wide,...  99.6 us
    unnamed x16, local copies, waits for them, and re-layouts  8.16 us

profile of v1, /device:TPU:8, one launch (start us, length us, event | category | flops | bytes accessed | tf_op | source)
XLA Modules:
  0.0 108.4 jit_solution(11626062312524049288)
XLA Ops:
  0.6 0.0 copy-start.4
  0.6 0.0 copy-start.5
  0.7 0.6 copy-done.4
  1.3 0.0 copy-done.5
  1.3 0.0 copy-start
  1.3 1.2 %copy-done = bf16[1,128,4096]{2,1,0:T(8,128)(2,1)S(1)} copy-done((bf16[1,128,4096]{2,1,0:T(8,128)(2,1)S(1)}, bf16[1,128,4096]{2,1,0:T(8,128)(2,1)}, u32[]{:S(2)}) %copy-start) | copy-done | bytes 1048600
  2.5 0.0 copy-start.1
  2.5 1.2 %copy-done.1 = bf16[1,128,4096]{2,1,0:T(8,128)(2,1)S(1)} copy-done((bf16[1,128,4096]{2,1,0:T(8,128)(2,1)S(1)}, bf16[1,128,4096]{2,1,0:T(8,128)(2,1)}, u32[]{:S(2)}) %copy-start.1) | copy-done | bytes 1048600
  3.8 0.0 copy-start.2
  3.8 0.9 copy-done.2
  4.7 0.0 copy-start.3
  4.7 0.9 copy-done.3
  5.6 99.6 %tree_attention.1 = (bf16[128,4096]{1,0:T(8,128)(2,1)S(1)}, bf16[128,4096]{1,0:T(8,128)(2,1)S(1)}, bf16[128,512]{1,0:T(8,128)(2,1)S(1)}, bf16[128,512]{1,0:T(8,128)(2,1)S(1)}) custom-call(bf16[128,4096]{1,0:T(8,128)(2,1)S(1)} %bitcast.8, bf16[128,4096]{1,0:T(8,128)(2,1)S(1)} %bitcast.9, bf16[128,512]{1,0:T(8,128)(2,1)S(1)} %bitcast.12, ...), custom_call_target="tpu_custom_call" | custom-call | tf_op jit(solution)/shard_map/tree_attention/pallas_call | solution.py:440
  105.1 1.0 copy.14
  106.1 1.0 copy.15
  107.1 0.7 copy.16
  107.7 0.7 copy.17
Async XLA Ops:
  0.6 0.7 copy-start.4
  0.6 0.7 copy-start.5
  1.3 1.2 %copy-start = (bf16[1,128,4096]{2,1,0:T(8,128)(2,1)S(1)}, bf16[1,128,4096]{2,1,0:T(8,128)(2,1)}, u32[]{:S(2)}) copy-start(bf16[1,128,4096]{2,1,0:T(8,128)(2,1)} %param.6) | copy-start | bytes 3145732
  2.5 1.2 %copy-start.1 = (bf16[1,128,4096]{2,1,0:T(8,128)(2,1)S(1)}, bf16[1,128,4096]{2,1,0:T(8,128)(2,1)}, u32[]{:S(2)}) copy-start(bf16[1,128,4096]{2,1,0:T(8,128)(2,1)} %param.9) | copy-start | bytes 3145732
  3.8 0.9 copy-start.2
  4.7 0.9 copy-start.3

commit v2 on v1

v2 whole, which is shorter than its diff:
```python
import functools

import jax
import jax.numpy as jnp
from jax import lax
from jax.experimental import pallas as pl
from jax.experimental.pallas import tpu as pltpu
from jax.sharding import PartitionSpec as P

H = 32
KVH = 4
HD = 128
BLOCK = 128
RESP = 6
BACK = 4
SLOTS = BACK + 2
OWN = SLOTS - 1
COLS = 4
QUAD = 4
RATIO = H // KVH
PAIRS = RATIO // 2
WIDE = 2 * BLOCK
SCALE = HD ** (-0.5)
LOG2E = 1.4426950408889634
MASKED = -1e30
OUT_STRAIGHT = 1
BACK_STRAIGHT = 1
AHEAD = 2
FORCED = True
MESH = pl.DeviceIdType.MESH
NT = (((1,), (1,)), ((), ()))
NN = (((1,), (0,)), ((), ()))


def dot(a, b, dims=NN):
    return lax.dot_general(a, b, dims, preferred_element_type=jnp.float32)


def kernel(
    ctx,
    dp,
    q_hbm,
    c_hbm,
    k_hbm,
    v_hbm,
    rew_ref,
    len_ref,
    o_hbm,
    dq_hbm,
    dk_ref,
    dv_ref,
    o_ref,
    dq_ref,
    q_ref,
    c_ref,
    k_ref,
    v_ref,
    kv,
    kt,
    vt,
    acc,
    own,
    give,
    got,
    chain,
    help_got,
    stat,
    quad_got,
    line_got,
    load,
    store,
    fsend,
    frecv,
    rsend,
    gsend,
    grecv,
    hsend,
    hrecv,
    csend,
    crecv,
    qsend,
    qrecv,
    lsend,
    lrecv,
):
    me = lax.axis_index("ctx")
    end = ctx - 1
    my_dp = lax.axis_index("dp")
    quads = dp // QUAD
    upward = lax.rem(my_dp, 2) == 0

    loads = [
        pltpu.make_async_copy(src, dst, load.at[n])
        for n, (src, dst) in enumerate(
            ((k_hbm, k_ref), (v_hbm, v_ref), (q_hbm, q_ref), (c_hbm, c_ref))
        )
    ]
    for copy in loads:
        copy.start()

    barrier = pltpu.get_barrier_semaphore()

    def greet_ctx(d, carry):
        pl.semaphore_signal(
            barrier, inc=1, device_id={"ctx": lax.rem(me + d, ctx)}, device_id_type=MESH
        )
        return carry

    lax.fori_loop(1, ctx, greet_ctx, 0)
    greeted = ctx - 1
    quad_base = my_dp // QUAD * QUAD
    quad_at = my_dp - quad_base

    def quad_peer(d):
        return quad_base + lax.rem(quad_at + d, QUAD)

    def line_peer(d):
        return lax.rem(my_dp // QUAD + d, quads) * QUAD + quad_at

    if dp > 1:
        for d in range(1, QUAD):
            pl.semaphore_signal(barrier, inc=1, device_id={"dp": quad_peer(d)}, device_id_type=MESH)
        for d in range(1, quads):
            pl.semaphore_signal(barrier, inc=1, device_id={"dp": line_peer(d)}, device_id_type=MESH)
        greeted += QUAD - 1 + quads - 1

    def blank(slot):
        for g in range(KVH):
            kv[g, slot] = jnp.zeros((2, BLOCK, HD), jnp.bfloat16)

    @pl.when(me == 0)
    def _():
        blank(0)

    for k in range(1, BACK + 1):

        @pl.when(me <= k)
        def _():
            blank(OWN - k)

    mean = rew_ref[0, 0]
    for r in range(1, RESP):
        mean = mean + rew_ref[0, r]
    mean = mean * (1.0 / RESP)
    square = jnp.float32(0.0)
    advantage = jnp.float32(0.0)
    first = jnp.int32(1)
    start = jnp.int32(1)
    for r in range(RESP):
        centered = rew_ref[0, r] - mean
        square = square + centered * centered
        advantage = jnp.where(start <= me, centered, advantage)
        first = jnp.where(start <= me, start, first)
        start = start + len_ref[0, r]
    stat[0] = jnp.full((8, HD), square, jnp.float32)
    bias = [jnp.where(me >= 1, 0.0, MASKED).astype(jnp.float32)]
    for k in range(BACK, 0, -1):
        bias.append(jnp.where(me - k >= first, 0.0, MASKED).astype(jnp.float32))

    loads[0].wait()
    loads[1].wait()
    for g in range(KVH):
        kv[g, OWN, 0] = k_ref[:, g * HD : (g + 1) * HD]
        kv[g, OWN, 1] = v_ref[:, g * HD : (g + 1) * HD]

    pl.semaphore_wait(barrier, greeted)

    def remote(src, dst, send, recv, axis, target):
        return pltpu.make_async_remote_copy(
            src_ref=src,
            dst_ref=dst,
            send_sem=send,
            recv_sem=recv,
            device_id={axis: target},
            device_id_type=MESH,
        )

    def at(distance):
        return lax.rem(me + (distance + ctx), ctx)

    def begin(copy):
        copy.start()

    def left(copy):
        copy.wait_send()

    def key_copy(g, src_slot, dst_slot, send, distance):
        return remote(
            kv.at[g, src_slot], kv.at[g, dst_slot], send, frecv.at[g, dst_slot], "ctx", at(distance)
        )

    def arrive(g, slot):
        key_copy(g, OWN, slot, fsend.at[g, 0], 1).wait_recv()

    def sends(g):
        straight = g < OUT_STRAIGHT
        yield from ((me == 0, k, 0) for k in (1, 2, 3, COLS, 2 * COLS, 3 * COLS))
        yield (me >= 1) & (me + 1 < ctx), 1, OWN - 1
        yield (me >= 1) & (me + 4 < ctx), 4, OWN - 4
        yield (me >= 1) & (me + 3 < ctx), 3, OWN - 3
        yield (me >= 1) & (me + 2 < ctx) & straight, 2, OWN - 2

    def each_send(g, do):
        for n, (when, distance, slot) in enumerate(sends(g)):

            @pl.when(when)
            def _():
                do(key_copy(g, OWN, slot, fsend.at[g, n], distance))

    in_first = (me >= 1) & (me < COLS)
    line = lax.rem(me, COLS)
    if FORCED:
        pass_up = (me >= 2) & (line <= 2) & ((line == 2) | upward)
        pass_down = (me >= COLS + 1) & (line >= 1) & ((line == 1) | jnp.logical_not(upward))
        by_next = (line == COLS - 1) | ((line >= 1) & upward)
    else:
        pass_up = (me >= 2) & (me < end) & (upward | (me == end - 1))
        pass_down = (me >= COLS) & jnp.logical_not(upward)
        by_next = upward | (me == end)

    def each_prompt(g, do):
        @pl.when(in_first)
        def _():
            for n in range(3):
                do(key_copy(g, 0, 0, rsend.at[g, n], (n + 1) * COLS))

    passes = (
        (pass_up, OWN - 1, OWN - 2, 1, 3),
        (pass_down, OWN - 3, OWN - 2, -1, 4),
    )

    def each_pass(g, do, ready):
        for when, here, there, distance, n in passes:

            @pl.when(when)
            def _():
                if ready:
                    arrive(g, here)
                do(key_copy(g, here, there, rsend.at[g, n], distance))

    def relay_prompt(g):
        @pl.when(in_first)
        def _():
            arrive(g, 0)

        each_prompt(g, begin)

    def await_keys(g):
        @pl.when(me >= COLS)
        def _():
            arrive(g, 0)

        later = g >= OUT_STRAIGHT
        for k, passed in ((1, pass_up), (2, None), (3, pass_down), (4, None)):
            when = me > k
            if passed is not None:
                when = when & jnp.logical_not(passed & later)

            @pl.when(when)
            def _():
                arrive(g, OWN - k)

    def quad_copy(d):
        return remote(
            stat.at[0], quad_got.at[d - 1], qsend.at[d - 1], qrecv.at[d - 1], "dp", quad_peer(d)
        )

    def line_copy(d):
        return remote(
            stat.at[1], line_got.at[d - 1], lsend.at[d - 1], lrecv.at[d - 1], "dp", line_peer(d)
        )

    if dp > 1:
        for d in range(1, QUAD):
            quad_copy(d).start()
    each_send(0, begin)
    if dp > 1:
        for d in range(1, QUAD):
            quad_copy(d).wait()
        part = stat[0]
        for d in range(1, QUAD):
            part = part + quad_got[d - 1]
        stat[1] = part
    relay_prompt(0)
    for g in range(1, AHEAD):
        each_send(g, begin)
    if dp > 1:
        for d in range(1, quads):
            line_copy(d).start()
    loads[2].wait()
    loads[3].wait()

    def weigh():
        if dp > 1:
            for d in range(1, quads):
                line_copy(d).wait()
            total = stat[1]
            for d in range(1, quads):
                total = total + line_got[d - 1]
        else:
            total = stat[0]
        stat[2] = advantage / jnp.sqrt(total * (1.0 / (dp * RESP)) + 1e-06)

    def grad_copy(g, k):
        return remote(
            give.at[g, OWN - k], got.at[g, k - 1], gsend.at[g, k - 1], grecv.at[g, k - 1], "ctx", at(-k)
        )

    def help_copy(g, n):
        return remote(
            give.at[g, OWN - 2],
            help_got.at[g, n],
            hsend.at[g],
            hrecv.at[g, n],
            "ctx",
            at(1 if n else -1),
        )

    def chain_copy(g, n):
        return remote(
            give.at[g, 0], chain.at[g, n], csend.at[g], crecv.at[g, n], "ctx", at(-(n + 1) * COLS)
        )

    def home_copy(g, k):
        return remote(
            give.at[g, 0], got.at[g, k - 1], csend.at[g], grecv.at[g, k - 1], "ctx", at(-k)
        )

    def each_chain(g, do):
        for n in range(3):

            @pl.when((me >= (n + 1) * COLS) & (me < (n + 2) * COLS))
            def _():
                do(chain_copy(g, n))

    def each_home(g, do):
        for k in range(1, COLS):

            @pl.when(me == k)
            def _():
                do(home_copy(g, k))

    def give_next(g, do, when):
        @pl.when((me > 1) & when)
        def _():
            do(grad_copy(g, 1))

    def give_third(g, do, when):
        @pl.when((me > 3) & when)
        def _():
            do(grad_copy(g, 3))

    def give_fourth(g, do):
        @pl.when(me > 4)
        def _():
            do(grad_copy(g, 4))

    def give_second(g, do):
        @pl.when((me > 2) & back_straight(g))
        def _():
            do(grad_copy(g, 2))

        @pl.when((me > 2) & jnp.logical_not(back_straight(g)) & by_next)
        def _():
            do(help_copy(g, 0))

        @pl.when((me > 2) & jnp.logical_not(back_straight(g)) & jnp.logical_not(by_next))
        def _():
            do(help_copy(g, 1))

    def give_first(g):
        alone = back_straight(g)
        give_second(g, begin)
        give_next(g, begin, alone | jnp.logical_not(pass_up))
        give_third(g, begin, alone | jnp.logical_not(pass_down))
        each_chain(g, begin)
        give_fourth(g, begin)

    def back_straight(g):
        return g >= KVH - BACK_STRAIGHT

    def add_to_give(g, slot, parts):
        total = give[g, slot].astype(jnp.float32)
        for part in parts:
            total = total + part.astype(jnp.float32)
        give[g, slot] = total.astype(jnp.bfloat16)

    def assist(g):
        @pl.when(pass_up)
        def _():
            help_copy(g, 0).wait_recv()
            add_to_give(g, OWN - 1, [help_got[g, 0]])

        give_next(g, begin, pass_up)

        @pl.when(pass_down)
        def _():
            help_copy(g, 1).wait_recv()
            add_to_give(g, OWN - 3, [help_got[g, 1]])

        give_third(g, begin, pass_down)

    def assist_prompt(g):
        @pl.when(in_first)
        def _():
            for n in range(3):
                chain_copy(g, n).wait_recv()
            add_to_give(g, 0, [chain[g, n] for n in range(3)])

        each_home(g, begin)

    row = lax.broadcasted_iota(jnp.int32, (BLOCK, WIDE), 0)
    column = lax.broadcasted_iota(jnp.int32, (BLOCK, WIDE), 1)
    causal = row <= lax.rem(column, BLOCK)

    def pair_step(g, pair):
        base = pl.multiple_of(g * (RATIO * HD) + pair * WIDE, WIDE)
        left_half = pl.ds(base, HD)
        right_half = pl.ds(pl.multiple_of(base + HD, HD), HD)
        query = jnp.concatenate([q_ref[:, left_half], q_ref[:, right_half]], axis=0)
        cot = jnp.concatenate([c_ref[:, left_half], c_ref[:, right_half]], axis=0)
        keys = kv[g, :, 0].reshape(SLOTS * BLOCK, HD)
        values = kv[g, :, 1].reshape(SLOTS * BLOCK, HD)
        raw = dot(keys, query, NT) * (SCALE * LOG2E)
        tiles = [raw[s * BLOCK : (s + 1) * BLOCK] + bias[s] for s in range(OWN)]
        tiles.append(jnp.where(causal, raw[OWN * BLOCK :], MASKED))
        scores = jnp.concatenate(tiles, axis=0)
        peak = jnp.max(scores, axis=0, keepdims=True)
        exps = jnp.exp2(scores - peak)
        probs = exps * (1.0 / jnp.sum(exps, axis=0, keepdims=True))
        low = probs.astype(jnp.bfloat16)
        dprobs = dot(values, cot, NT)
        delta = jnp.sum(probs * dprobs, axis=0, keepdims=True)
        dscores = (probs * (dprobs - delta)).astype(jnp.bfloat16)
        attn = dot(vt[...], low)
        qgrad = dot(kt[...], dscores) * SCALE
        acc[0] += dot(dscores, query)
        acc[1] += dot(low, cot)
        o_ref[:, left_half] = attn[:, :HD].T.astype(jnp.bfloat16)
        o_ref[:, right_half] = attn[:, HD:].T.astype(jnp.bfloat16)
        dq_ref[:, left_half] = qgrad[:, :HD].T.astype(jnp.bfloat16)
        dq_ref[:, right_half] = qgrad[:, HD:].T.astype(jnp.bfloat16)

    def stores(g):
        heads = pl.ds(pl.multiple_of(g * (RATIO * HD), RATIO * HD), RATIO * HD)
        return [
            pltpu.make_async_copy(src.at[:, heads], dst.at[:, heads], store.at[g, n])
            for n, (src, dst) in enumerate(((o_ref, o_hbm), (dq_ref, dq_hbm)))
        ]

    def group_step(g, carry):
        await_keys(g)
        kt[...] = kv[g, :, 0].reshape(SLOTS * BLOCK, HD).T
        vt[...] = kv[g, :, 1].reshape(SLOTS * BLOCK, HD).T
        acc[...] = jnp.zeros_like(acc)

        def halves(half, inner):
            @pl.when((half == 0) & (g < KVH - AHEAD))
            def _():
                each_send(g + AHEAD, begin)

            @pl.when((half == 1) & (g < KVH - 1))
            def _():
                relay_prompt(g + 1)

            @pl.when((half == 1) & (g < KVH - 1) & (g + 1 >= OUT_STRAIGHT))
            def _():
                each_pass(g + 1, begin, True)

            @pl.when((half == 1) & (g > 0) & jnp.logical_not(back_straight(g - 1)))
            def _():
                assist(g - 1)

            @pl.when((half == 1) & (g > 0))
            def _():
                assist_prompt(g - 1)

            for n in range(PAIRS // 2):
                pair_step(g, half * (PAIRS // 2) + n)
            return inner

        lax.fori_loop(0, 2, halves, 0)

        @pl.when(g == 0)
        def _():
            weigh()

        weight = stat[2, 0:1, :]
        scale = weight * SCALE
        for s in range(OWN):
            rows = pl.ds(s * BLOCK, BLOCK)
            give[g, s, 0] = (acc[0, rows, :] * scale).astype(jnp.bfloat16)
            give[g, s, 1] = (acc[1, rows, :] * weight).astype(jnp.bfloat16)
        rows = pl.ds(OWN * BLOCK, BLOCK)
        own[g, 0] = acc[0, rows, :] * scale
        own[g, 1] = acc[1, rows, :] * weight
        give_first(g)
        for n in range(RATIO):
            head = pl.ds(pl.multiple_of(g * (RATIO * HD) + n * HD, HD), HD)
            dq_ref[:, head] = (dq_ref[:, head].astype(jnp.float32) * weight).astype(jnp.bfloat16)
        for copy in stores(g):
            copy.start()
        return carry

    lax.fori_loop(0, KVH, group_step, 0)
    assist_prompt(KVH - 1)

    def close_group(g, carry):
        def add(part):
            own[g] += part.astype(jnp.float32)

        for k in range(1, BACK + 1):
            here = (me >= 1) & (me + k < ctx)
            if k == 2:
                here = here & back_straight(g)
            if k < COLS:
                here = here | (me == 0)

            @pl.when(here)
            def _():
                grad_copy(g, k).wait_recv()
                add(got[g, k - 1])

        @pl.when(me == 0)
        def _():
            for n in range(3):
                chain_copy(g, n).wait_recv()
                add(chain[g, n])

        place = pl.ds(pl.multiple_of(g * HD, HD), HD)
        dk_ref[:, place] = own[g, 0].astype(jnp.bfloat16)
        dv_ref[:, place] = own[g, 1].astype(jnp.bfloat16)
        return carry

    lax.fori_loop(0, KVH, close_group, 0)

    def settle(g, carry):
        each_send(g, left)
        each_prompt(g, left)

        @pl.when(g >= OUT_STRAIGHT)
        def _():
            each_pass(g, left, False)

        for copy in stores(g):
            copy.wait()
        give_second(g, left)
        give_next(g, left, True)
        give_third(g, left, True)
        give_fourth(g, left)
        each_chain(g, left)
        each_home(g, left)
        return carry

    lax.fori_loop(0, KVH, settle, 0)


def place(*refs):
    sources, targets, parts, sems = refs[:4], refs[4:8], refs[8:12], refs[12]
    loads, stores = [], []
    for n in range(4):
        rows = BLOCK // 4 if n < 2 else BLOCK
        for c in range(BLOCK // rows):
            span = pl.ds(c * rows, rows)
            loads.append(
                pltpu.make_async_copy(sources[n].at[span], parts[n].at[span], sems.at[0, n, c])
            )
            stores.append(
                pltpu.make_async_copy(parts[n].at[span], targets[n].at[span], sems.at[1, n, c])
            )
    for copy in loads:
        copy.start()
    for load, store in zip(loads, stores):
        load.wait()
        store.start()
    for copy in stores:
        copy.wait()


def body(queries, keys, values, out_cotangent, rewards, lengths):
    ctx = lax.axis_size("ctx")
    dp = lax.axis_size("dp")
    tokens = queries.shape[1]
    vmem = pl.BlockSpec(memory_space=pltpu.VMEM)
    smem = pl.BlockSpec(memory_space=pltpu.SMEM)
    hbm = pl.BlockSpec(memory_space=pl.ANY)
    wide = jax.ShapeDtypeStruct((tokens, H * HD), jnp.bfloat16)
    thin = jax.ShapeDtypeStruct((tokens, KVH * HD), jnp.bfloat16)
    block = (2, BLOCK, HD)
    quads = max(dp // QUAD - 1, 1)
    dma = pltpu.SemaphoreType.DMA
    outs = pl.pallas_call(
        functools.partial(kernel, ctx, dp),
        out_shape=(wide, wide, thin, thin),
        in_specs=[hbm] * 4 + [smem] * 2,
        out_specs=(hbm, hbm, vmem, vmem),
        scratch_shapes=[
            pltpu.VMEM(wide.shape, jnp.bfloat16),
            pltpu.VMEM(wide.shape, jnp.bfloat16),
            pltpu.VMEM(wide.shape, jnp.bfloat16),
            pltpu.VMEM(wide.shape, jnp.bfloat16),
            pltpu.VMEM(thin.shape, jnp.bfloat16),
            pltpu.VMEM(thin.shape, jnp.bfloat16),
            pltpu.VMEM((KVH, SLOTS) + block, jnp.bfloat16),
            pltpu.VMEM((HD, SLOTS * BLOCK), jnp.bfloat16),
            pltpu.VMEM((HD, SLOTS * BLOCK), jnp.bfloat16),
            pltpu.VMEM((2, SLOTS * BLOCK, HD), jnp.float32),
            pltpu.VMEM((KVH,) + block, jnp.float32),
            pltpu.VMEM((KVH, OWN) + block, jnp.bfloat16),
            pltpu.VMEM((KVH, BACK) + block, jnp.bfloat16),
            pltpu.VMEM((KVH, 3) + block, jnp.bfloat16),
            pltpu.VMEM((KVH, 2) + block, jnp.bfloat16),
            pltpu.VMEM((3, 8, HD), jnp.float32),
            pltpu.VMEM((QUAD - 1, 8, HD), jnp.float32),
            pltpu.VMEM((quads, 8, HD), jnp.float32),
            dma((4,)),
            dma((KVH, 2)),
            dma((KVH, BACK + 6)),
            dma((KVH, SLOTS)),
            dma((KVH, 5)),
            dma((KVH, BACK)),
            dma((KVH, BACK)),
            dma((KVH,)),
            dma((KVH, 2)),
            dma((KVH,)),
            dma((KVH, 3)),
            dma((QUAD - 1,)),
            dma((QUAD - 1,)),
            dma((quads,)),
            dma((quads,)),
        ],
        compiler_params=pltpu.CompilerParams(
            collective_id=0, has_side_effects=True, vmem_limit_bytes=61 * 1024 * 1024
        ),
        name="tree_attention",
    )(queries[0], out_cotangent[0], keys[0], values[0], rewards, lengths)
    outs = pl.pallas_call(
        place,
        out_shape=(wide, wide, thin, thin),
        in_specs=[hbm] * 4,
        out_specs=(hbm,) * 4,
        scratch_shapes=[pltpu.VMEM(out.shape, out.dtype) for out in (wide, wide, thin, thin)]
        + [dma((2, 4, 4))],
        compiler_params=pltpu.CompilerParams(vmem_limit_bytes=61 * 1024 * 1024),
        name="place_results",
    )(*outs)
    return tuple(out[None] for out in outs)


def solution(mesh):
    placed = (P("dp", "ctx", None),) * 4
    return jax.shard_map(
        body,
        mesh=mesh,
        in_specs=placed + (P("dp", None),) * 2,
        out_specs=placed,
        check_vma=False,
    )
```

time: 109 us -> 78.6 us (0.72)
  the two profiles are of different devices: /device:TPU:8 before, /device:TPU:392 now
where the time goes in v2:
time: 78.6 us; the launch traced here: 78.4 us
  Pallas kernels  77.8 us (99%)
    pallas_call x1, Pallas kernels, body(): pl.pallas_call(functools.partial(kernel, ctx, dp), out_shape=(wide, wide,...  75.1 us
    pallas_call x1, Pallas kernels, body(): pl.pallas_call(place, out_shape=(wide, wide, thin, thin), in_specs=[hbm]...  2.62 us

profile of v2, /device:TPU:392, one launch (start us, length us, event | category | flops | bytes accessed | tf_op | source)
XLA Modules:
  0.0 78.4 jit_solution(2175297324328442259)
XLA Ops:
  0.6 75.1 %tree_attention.1 = (bf16[128,4096]{1,0:T(8,128)(2,1)}, bf16[128,4096]{1,0:T(8,128)(2,1)}, bf16[128,512]{1,0:T(8,128)(2,1)}, bf16[128,512]{1,0:T(8,128)(2,1)}) custom-call(bf16[128,4096]{1,0:T(8,128)(2,1)} %bitcast.8, bf16[128,4096]{1,0:T(8,128)(2,1)} %bitcast.9, bf16[128,512]{1,0:T(8,128)(2,1)} %bitcast.10, bf16[128,512]{1,0:T(8,128)(2,1)} %bitcast.11, ...), custom_call_target="tpu_custom_call" | custom-call | tf_op jit(solution)/shard_map/tree_attention/pallas_call | solution.py:592
  75.8 2.6 %place_results.1 = (bf16[128,4096]{1,0:T(8,128)(2,1)}, bf16[128,4096]{1,0:T(8,128)(2,1)}, bf16[128,512]{1,0:T(8,128)(2,1)}, bf16[128,512]{1,0:T(8,128)(2,1)}) custom-call(bf16[128,4096]{1,0:T(8,128)(2,1)} %get-tuple-element.12.refs_0_, bf16[128,4096]{1,0:T(8,128)(2,1)} %get-tuple-element.13.refs_1_, bf16[128,512]{1,0:T(8,128)(2,1)} %get-tuple-element.14.refs_2_, ...), custom_call_target="tpu_custom_call" | custom-call | tf_op jit(solution)/shard_map/place_results/pallas_call | solution.py:637

commit v3 on v2

--- a/solution.py
+++ b/solution.py
@@ -23,10 +23,8 @@
 SCALE = HD ** (-0.5)
 LOG2E = 1.4426950408889634
 MASKED = -1e30
-OUT_STRAIGHT = 1
-BACK_STRAIGHT = 1
-AHEAD = 2
-FORCED = True
+SEND_ORDER = (1, 4, 3, 2)
+BACK_ORDER = (2, 1, 3, 4)
 MESH = pl.DeviceIdType.MESH
 NT = (((1,), (1,)), ((), ()))
 NN = (((1,), (0,)), ((), ()))
@@ -63,7 +61,6 @@
     give,
     got,
     chain,
-    help_got,
     stat,
     quad_got,
     line_got,
@@ -74,8 +71,6 @@
     rsend,
     gsend,
     grecv,
-    hsend,
-    hrecv,
     csend,
     crecv,
     qsend,
@@ -87,7 +82,6 @@
     end = ctx - 1
     my_dp = lax.axis_index("dp")
     quads = dp // QUAD
-    upward = lax.rem(my_dp, 2) == 0
 
     loads = [
         pltpu.make_async_copy(src, dst, load.at[n])
@@ -193,12 +187,10 @@
         key_copy(g, OWN, slot, fsend.at[g, 0], 1).wait_recv()
 
     def sends(g):
-        straight = g < OUT_STRAIGHT
         yield from ((me == 0, k, 0) for k in (1, 2, 3, COLS, 2 * COLS, 3 * COLS))
-        yield (me >= 1) & (me + 1 < ctx), 1, OWN - 1
-        yield (me >= 1) & (me + 4 < ctx), 4, OWN - 4
-        yield (me >= 1) & (me + 3 < ctx), 3, OWN - 3
-        yield (me >= 1) & (me + 2 < ctx) & straight, 2, OWN - 2
+        for k in SEND_ORDER:
+            when = (me >= 1) & (me + k < ctx)
+            yield when, k, OWN - k
 
     def each_send(g, do):
         for n, (when, distance, slot) in enumerate(sends(g)):
@@ -208,15 +200,6 @@
                 do(key_copy(g, OWN, slot, fsend.at[g, n], distance))
 
     in_first = (me >= 1) & (me < COLS)
-    line = lax.rem(me, COLS)
-    if FORCED:
-        pass_up = (me >= 2) & (line <= 2) & ((line == 2) | upward)
-        pass_down = (me >= COLS + 1) & (line >= 1) & ((line == 1) | jnp.logical_not(upward))
-        by_next = (line == COLS - 1) | ((line >= 1) & upward)
-    else:
-        pass_up = (me >= 2) & (me < end) & (upward | (me == end - 1))
-        pass_down = (me >= COLS) & jnp.logical_not(upward)
-        by_next = upward | (me == end)
 
     def each_prompt(g, do):
         @pl.when(in_first)
@@ -224,20 +207,6 @@
             for n in range(3):
                 do(key_copy(g, 0, 0, rsend.at[g, n], (n + 1) * COLS))
 
-    passes = (
-        (pass_up, OWN - 1, OWN - 2, 1, 3),
-        (pass_down, OWN - 3, OWN - 2, -1, 4),
-    )
-
-    def each_pass(g, do, ready):
-        for when, here, there, distance, n in passes:
-
-            @pl.when(when)
-            def _():
-                if ready:
-                    arrive(g, here)
-                do(key_copy(g, here, there, rsend.at[g, n], distance))
-
     def relay_prompt(g):
         @pl.when(in_first)
         def _():
@@ -250,12 +219,8 @@
         def _():
             arrive(g, 0)
 
-        later = g >= OUT_STRAIGHT
-        for k, passed in ((1, pass_up), (2, None), (3, pass_down), (4, None)):
+        for k in range(1, BACK + 1):
             when = me > k
-            if passed is not None:
-                when = when & jnp.logical_not(passed & later)
-
             @pl.when(when)
             def _():
                 arrive(g, OWN - k)
@@ -282,7 +247,7 @@
             part = part + quad_got[d - 1]
         stat[1] = part
     relay_prompt(0)
-    for g in range(1, AHEAD):
+    for g in range(1, KVH):
         each_send(g, begin)
     if dp > 1:
         for d in range(1, quads):
@@ -306,16 +271,6 @@
             give.at[g, OWN - k], got.at[g, k - 1], gsend.at[g, k - 1], grecv.at[g, k - 1], "ctx", at(-k)
         )
 
-    def help_copy(g, n):
-        return remote(
-            give.at[g, OWN - 2],
-            help_got.at[g, n],
-            hsend.at[g],
-            hrecv.at[g, n],
-            "ctx",
-            at(1 if n else -1),
-        )
-
     def chain_copy(g, n):
         return remote(
             give.at[g, 0], chain.at[g, n], csend.at[g], crecv.at[g, n], "ctx", at(-(n + 1) * COLS)
@@ -340,65 +295,22 @@
             def _():
                 do(home_copy(g, k))
 
-    def give_next(g, do, when):
-        @pl.when((me > 1) & when)
-        def _():
-            do(grad_copy(g, 1))
-
-    def give_third(g, do, when):
-        @pl.when((me > 3) & when)
-        def _():
-            do(grad_copy(g, 3))
-
-    def give_fourth(g, do):
-        @pl.when(me > 4)
-        def _():
-            do(grad_copy(g, 4))
-
-    def give_second(g, do):
-        @pl.when((me > 2) & back_straight(g))
-        def _():
-            do(grad_copy(g, 2))
-
-        @pl.when((me > 2) & jnp.logical_not(back_straight(g)) & by_next)
-        def _():
-            do(help_copy(g, 0))
-
-        @pl.when((me > 2) & jnp.logical_not(back_straight(g)) & jnp.logical_not(by_next))
-        def _():
-            do(help_copy(g, 1))
+    def each_grad(g, do):
+        for k in BACK_ORDER:
+
+            @pl.when(me > k)
+            def _():
+                do(grad_copy(g, k))
 
     def give_first(g):
-        alone = back_straight(g)
-        give_second(g, begin)
-        give_next(g, begin, alone | jnp.logical_not(pass_up))
-        give_third(g, begin, alone | jnp.logical_not(pass_down))
         each_chain(g, begin)
-        give_fourth(g, begin)
-
-    def back_straight(g):
-        return g >= KVH - BACK_STRAIGHT
+        each_grad(g, begin)
 
     def add_to_give(g, slot, parts):
         total = give[g, slot].astype(jnp.float32)
         for part in parts:
             total = total + part.astype(jnp.float32)
         give[g, slot] = total.astype(jnp.bfloat16)
-
-    def assist(g):
-        @pl.when(pass_up)
-        def _():
-            help_copy(g, 0).wait_recv()
-            add_to_give(g, OWN - 1, [help_got[g, 0]])
-
-        give_next(g, begin, pass_up)
-
-        @pl.when(pass_down)
-        def _():
-            help_copy(g, 1).wait_recv()
-            add_to_give(g, OWN - 3, [help_got[g, 1]])
-
-        give_third(g, begin, pass_down)
 
     def assist_prompt(g):
         @pl.when(in_first)
@@ -454,32 +366,16 @@
         vt[...] = kv[g, :, 1].reshape(SLOTS * BLOCK, HD).T
         acc[...] = jnp.zeros_like(acc)
 
-        def halves(half, inner):
-            @pl.when((half == 0) & (g < KVH - AHEAD))
-            def _():
-                each_send(g + AHEAD, begin)
-
-            @pl.when((half == 1) & (g < KVH - 1))
-            def _():
-                relay_prompt(g + 1)
-
-            @pl.when((half == 1) & (g < KVH - 1) & (g + 1 >= OUT_STRAIGHT))
-            def _():
-                each_pass(g + 1, begin, True)
-
-            @pl.when((half == 1) & (g > 0) & jnp.logical_not(back_straight(g - 1)))
-            def _():
-                assist(g - 1)
-
-            @pl.when((half == 1) & (g > 0))
-            def _():
-                assist_prompt(g - 1)
-
-            for n in range(PAIRS // 2):
-                pair_step(g, half * (PAIRS // 2) + n)
-            return inner
-
-        lax.fori_loop(0, 2, halves, 0)
+        for n in range(PAIRS):
+            pair_step(g, n)
+
+        @pl.when(g < KVH - 1)
+        def _():
+            relay_prompt(g + 1)
+
+        @pl.when(g > 0)
+        def _():
+            assist_prompt(g - 1)
 
         @pl.when(g == 0)
         def _():
@@ -511,8 +407,6 @@
 
         for k in range(1, BACK + 1):
             here = (me >= 1) & (me + k < ctx)
-            if k == 2:
-                here = here & back_straight(g)
             if k < COLS:
                 here = here | (me == 0)
 
@@ -538,16 +432,9 @@
         each_send(g, left)
         each_prompt(g, left)
 
-        @pl.when(g >= OUT_STRAIGHT)
-        def _():
-            each_pass(g, left, False)
-
         for copy in stores(g):
             copy.wait()
-        give_second(g, left)
-        give_next(g, left, True)
-        give_third(g, left, True)
-        give_fourth(g, left)
+        each_grad(g, left)
         each_chain(g, left)
         each_home(g, left)
         return carry
@@ -609,7 +496,6 @@
             pltpu.VMEM((KVH, OWN) + block, jnp.bfloat16),
             pltpu.VMEM((KVH, BACK) + block, jnp.bfloat16),
             pltpu.VMEM((KVH, 3) + block, jnp.bfloat16),
-            pltpu.VMEM((KVH, 2) + block, jnp.bfloat16),
             pltpu.VMEM((3, 8, HD), jnp.float32),
             pltpu.VMEM((QUAD - 1, 8, HD), jnp.float32),
             pltpu.VMEM((quads, 8, HD), jnp.float32),
@@ -617,11 +503,9 @@
             dma((KVH, 2)),
             dma((KVH, BACK + 6)),
             dma((KVH, SLOTS)),
-            dma((KVH, 5)),
+            dma((KVH, 3)),
             dma((KVH, BACK)),
             dma((KVH, BACK)),
-            dma((KVH,)),
-            dma((KVH, 2)),
             dma((KVH,)),
             dma((KVH, 3)),
             dma((QUAD - 1,)),

time: 78.6 us -> 74.2 us (0.944)
  the two profiles are of different devices: /device:TPU:392 before, /device:TPU:64 now
where the time goes in v3:
time: 74.2 us; the launch traced here: 74 us
  Pallas kernels  73.4 us (99%)
    pallas_call x1, Pallas kernels, body(): pl.pallas_call(functools.partial(kernel, ctx, dp), out_shape=(wide, wide,...  70.8 us
    pallas_call x1, Pallas kernels, body(): pl.pallas_call(place, out_shape=(wide, wide, thin, thin), in_specs=[hbm]...  2.62 us

profile of v3, /device:TPU:64, one launch (start us, length us, event | category | flops | bytes accessed | tf_op | source)
XLA Modules:
  0.0 74.0 jit_solution(16648558973625481421)
XLA Ops:
  0.6 70.8 %tree_attention.1 = (bf16[128,4096]{1,0:T(8,128)(2,1)}, bf16[128,4096]{1,0:T(8,128)(2,1)}, bf16[128,512]{1,0:T(8,128)(2,1)}, bf16[128,512]{1,0:T(8,128)(2,1)}) custom-call(bf16[128,4096]{1,0:T(8,128)(2,1)} %bitcast.8, bf16[128,4096]{1,0:T(8,128)(2,1)} %bitcast.9, bf16[128,512]{1,0:T(8,128)(2,1)} %bitcast.10, bf16[128,512]{1,0:T(8,128)(2,1)} %bitcast.11, ...), custom_call_target="tpu_custom_call" | custom-call | tf_op jit(solution)/shard_map/tree_attention/pallas_call | solution.py:479
  71.4 2.6 %place_results.1 = (bf16[128,4096]{1,0:T(8,128)(2,1)}, bf16[128,4096]{1,0:T(8,128)(2,1)}, bf16[128,512]{1,0:T(8,128)(2,1)}, bf16[128,512]{1,0:T(8,128)(2,1)}) custom-call(bf16[128,4096]{1,0:T(8,128)(2,1)} %get-tuple-element.12.refs_0_, bf16[128,4096]{1,0:T(8,128)(2,1)} %get-tuple-element.13.refs_1_, bf16[128,512]{1,0:T(8,128)(2,1)} %get-tuple-element.14.refs_2_, ...), custom_call_target="tpu_custom_call" | custom-call | tf_op jit(solution)/shard_map/place_results/pallas_call | solution.py:521
